TPU v7x, 32 devices: a whole 2x2x4 slice. The times are simulated.
32 devices in a mesh: groups: 2 (over x), pool: 16 (over z, y, core).
Axes of the slice: x: 2, y: 2, z: 4, core: 2. Of those that a mesh axis runs over, the one named last changes fastest.
Arguments:
- hidden: bfloat16 [2, 32, 8192], P(None, 'groups', 'pool'), parts along dimension 1, may hold values from -6 to 6
- norm_gain_vector: float32 [8192], replicated, may hold values from 0.1 to 1.9
- query_key_value_weight: bfloat16 [8192, 10240], P('pool'), may hold values from -0.0625 to 0.0625
- output_weight: bfloat16 [8192, 8192], P(None, 'pool'), may hold values from -0.0625 to 0.0625
- key_value_cache: bfloat16 [32, 256, 2048], P(('groups', 'pool')), parts along dimension 0, may hold values from -60 to 60
- cache_valid_length: int32 [32], P(('groups', 'pool')), parts along dimension 0, may hold values from 1 to 256, as said below
- request_adapter_index: int32 [2, 32, 1], P(None, 'groups'), parts along dimension 1, may hold values from 0 to 15
- adapter_slot_place: int32 [32], P('groups'), parts along dimension 0, may hold values from 0 to 15, each once
- adapter_rank_used: int32 [32], P('groups'), parts along dimension 0, may hold values from 4 to 16, as said below
- adapter_down_factor: float32 [32, 48, 8192], P(('groups', 'pool')), parts along dimension 0, may hold values from -0.0625 to 0.0625
- query_up_factor: float32 [32, 16, 8192], P(('groups', 'pool')), parts along dimension 0, may hold values from -1.5 to 1.5
- key_value_up_factor: float32 [32, 2, 16, 1024], P(('groups', 'pool')), parts along dimension 0, may hold values from -1.5 to 1.5
- output_down_factor: float32 [32, 16, 8192], P(('groups', 'pool')), parts along dimension 0, may hold values from -0.0625 to 0.0625
- output_up_factor: float32 [32, 16, 8192], P(('groups', 'pool')), parts along dimension 0, may hold values from -1.5 to 1.5
Outputs:
- block_out: bfloat16 [2, 32, 8192], P(None, 'groups', 'pool'), parts along dimension 1
- new_kv: bfloat16 [2, 32, 2048], P(None, ('groups', 'pool')), parts along dimension 1
There are 2 independent parts, one for each index of `groups`. A program takes and returns all parts, laid end to end along the dimension named above; an argument that names none is the same for every part. Nothing has to cross between parts.
Inputs may be any that keep to these rules, and one draw needn't show every extreme that they name: `cache_valid_length`: one request in every draw has all 256 positions valid. `adapter_rank_used`: factor rows at or beyond an adapter's rank are not used; some adapter has rank 16.
All inputs are finite; a program needn't handle non-finite values.
Results may differ from a plain program's by a relative error of at most 0.012.
The roundings to bfloat16 on the way count: a program that leaves them out, or rounds other values in their place, can miss the bound.
Values may be sent and summed in bfloat16 or wider, within the bound.
A program may use at most 128 MiB of HBM per device.

v0:
```python
import jax
import jax.numpy as jnp
from jax import lax
from jax.sharding import PartitionSpec as P

HEADS = 64
KV_HEADS = 8
HEAD_DIM = 128


epsilon = 1e-05
highest_precision = lax.Precision.HIGHEST


def lookup(lookup_table, lookup_index):
    matches = lookup_index[:, None] == jnp.arange(lookup_table.shape[0], dtype=jnp.int32)[None, :]
    return jnp.sum(jnp.where(matches, lookup_table[None, :], 0), axis=1)


def widen_rows(slot_onehot, shrunk_rows, factors):
    spread = (slot_onehot[:, :, None] * shrunk_rows[:, None, :]).reshape(slot_onehot.shape[0], -1)
    return jnp.dot(
        spread, factors.reshape(spread.shape[1], factors.shape[-1]), precision=highest_precision
    )


def attend_block(queries, cache_rows, lengths, fresh_kv):
    kv_width = KV_HEADS * HEAD_DIM
    group_size = HEADS // KV_HEADS
    score_scale = HEAD_DIM ** (-0.5)
    batch_rows, positions = (cache_rows.shape[0], cache_rows.shape[1])
    fresh_count = fresh_kv.shape[1]
    query_heads = queries.reshape(batch_rows, KV_HEADS, group_size, HEAD_DIM)
    keys_cache = cache_rows[:, :, :kv_width].reshape(batch_rows, positions, KV_HEADS, HEAD_DIM)
    values_cache = cache_rows[:, :, kv_width:].reshape(batch_rows, positions, KV_HEADS, HEAD_DIM)
    keys_fresh = fresh_kv[:, :, :kv_width].reshape(batch_rows, fresh_count, KV_HEADS, HEAD_DIM)
    values_fresh = fresh_kv[:, :, kv_width:].reshape(batch_rows, fresh_count, KV_HEADS, HEAD_DIM)
    cache_scores = (
        jnp.einsum("rhgd,rchd->rhgc", query_heads, keys_cache, preferred_element_type=jnp.float32)
        * score_scale
    )
    valid_cache = jnp.arange(positions)[None, :] < lengths[:, None]
    cache_scores = jnp.where(valid_cache[:, None, None, :], cache_scores, -1e30)
    fresh_scores = (
        jnp.einsum("rhgd,rnhd->rhgn", query_heads, keys_fresh, preferred_element_type=jnp.float32)
        * score_scale
    )
    row_max = jnp.maximum(jnp.max(cache_scores, axis=-1), jnp.max(fresh_scores, axis=-1))
    cache_exp = jnp.exp(cache_scores - row_max[..., None])
    fresh_exp = jnp.exp(fresh_scores - row_max[..., None])
    total = jnp.sum(cache_exp, axis=-1) + jnp.sum(fresh_exp, axis=-1)
    cache_weights = (cache_exp / total[..., None]).astype(jnp.bfloat16)
    fresh_weights = (fresh_exp / total[..., None]).astype(jnp.bfloat16)
    result = jnp.einsum(
        "rhgc,rchd->rhgd", cache_weights, values_cache, preferred_element_type=jnp.float32
    )
    result = result + jnp.einsum(
        "rhgn,rnhd->rhgd", fresh_weights, values_fresh, preferred_element_type=jnp.float32
    )
    return result.reshape(batch_rows, HEADS * HEAD_DIM).astype(jnp.bfloat16)


def local(
    hidden,
    norm_gain_vector,
    query_key_value_weight,
    output_weight,
    key_value_cache,
    cache_valid_length,
    request_adapter_index,
    adapter_slot_place,
    adapter_rank_used,
    adapter_down_factor,
    query_up_factor,
    key_value_up_factor,
    output_down_factor,
    output_up_factor,
):
    position = lax.axis_index("pool")
    step_count, requests, width_dev = hidden.shape
    replica_slots = adapter_down_factor.shape[0]
    maximum_rank_size = query_up_factor.shape[1]
    query_feature_width = output_weight.shape[0]
    hidden_width_size = norm_gain_vector.shape[0]
    gain_slice = lax.dynamic_slice_in_dim(norm_gain_vector, position * width_dev, width_dev)
    gathered = lax.all_gather(hidden, "pool", axis=2, tiled=True)
    outputs = []
    entries = []
    for step_index in range(step_count):
        adapter_of = request_adapter_index[step_index, :, 0]
        slot_of = lookup(adapter_slot_place, adapter_of)
        rank_of = lookup(adapter_rank_used, adapter_of)
        factor = 4.0 / jnp.sqrt(rank_of.astype(jnp.float32))
        rank_keep = (jnp.arange(maximum_rank_size)[None, :] < rank_of[:, None]).astype(
            jnp.float32
        ) * factor[:, None]
        local_onehot_rows = (
            slot_of[:, None] == position * replica_slots + jnp.arange(replica_slots)[None, :]
        ).astype(jnp.float32)
        local_rows = hidden[step_index].astype(jnp.float32)
        whole_rows = gathered[step_index].astype(jnp.float32)
        inverse = lax.rsqrt(jnp.mean(whole_rows * whole_rows, axis=1) + epsilon)
        raw_shrink = jnp.dot(
            whole_rows * norm_gain_vector[None, :],
            adapter_down_factor.reshape(replica_slots * 3 * maximum_rank_size, hidden_width_size).T,
            precision=highest_precision,
        )
        raw_shrink = raw_shrink.reshape(requests, replica_slots, 3 * maximum_rank_size)
        shrunk_rows = jnp.sum(local_onehot_rows[:, :, None] * raw_shrink, axis=1) * inverse[:, None]
        shrunk_rows = shrunk_rows.reshape(requests, 3, maximum_rank_size) * rank_keep[:, None, :]
        normed = (local_rows * gain_slice[None, :] * inverse[:, None]).astype(jnp.bfloat16)
        query_update = widen_rows(local_onehot_rows, shrunk_rows[:, 0], query_up_factor)
        key_update = widen_rows(local_onehot_rows, shrunk_rows[:, 1], key_value_up_factor[:, 0])
        value_update = widen_rows(local_onehot_rows, shrunk_rows[:, 2], key_value_up_factor[:, 1])
        delta_qkv = jnp.concatenate([query_update, key_update, value_update], axis=1)
        mixed = lax.psum_scatter(
            jnp.dot(normed, query_key_value_weight, preferred_element_type=jnp.float32) + delta_qkv,
            "pool",
            scatter_dimension=0,
            tiled=True,
        )
        queries = mixed[:, :query_feature_width].astype(jnp.bfloat16)
        kv_entry = mixed[:, query_feature_width:].astype(jnp.bfloat16)
        entries.append(kv_entry)
        attention_result = attend_block(
            queries, key_value_cache, cache_valid_length, jnp.stack(entries, axis=1)
        )
        out_block_rows = lax.all_gather(attention_result, "pool", axis=0, tiled=True)
        base_part = jnp.dot(out_block_rows, output_weight, preferred_element_type=jnp.float32)
        own_part = jnp.dot(
            out_block_rows.astype(jnp.float32),
            output_down_factor.reshape(replica_slots * maximum_rank_size, query_feature_width).T,
            precision=highest_precision,
        )
        joined = jnp.concatenate([base_part, own_part], axis=1)
        base_out = joined[:, :width_dev]
        own_shrink = joined[:, width_dev:].reshape(requests, replica_slots, maximum_rank_size)
        output_shrink_rows = jnp.sum(local_onehot_rows[:, :, None] * own_shrink, axis=1) * rank_keep
        complete_update = widen_rows(local_onehot_rows, output_shrink_rows, output_up_factor)
        output_update = lax.psum_scatter(complete_update, "pool", scatter_dimension=1, tiled=True)
        outputs.append((local_rows + base_out + output_update).astype(jnp.bfloat16))
    return (jnp.stack(outputs), jnp.stack(entries))


def solution(mesh):
    placed = (
        P(None, "groups", "pool"),
        P(),
        P("pool", None),
        P(None, "pool"),
        P(("groups", "pool"), None, None),
        P(("groups", "pool")),
        P(None, "groups", None),
        P("groups"),
        P("groups"),
        P(("groups", "pool"), None, None),
        P(("groups", "pool"), None, None),
        P(("groups", "pool"), None, None, None),
        P(("groups", "pool"), None, None),
        P(("groups", "pool"), None, None),
    )
    return jax.shard_map(
        local,
        mesh=mesh,
        in_specs=placed,
        out_specs=(P(None, "groups", "pool"), P(None, ("groups", "pool"), None)),
        check_vma=False,
    )
```

profile of v0, /device:TPU:0, one launch (start us, length us, event | category | flops | bytes accessed | tf_op | source)
XLA Modules:
  0.0 282.5 jit_solution(12852564670989956509)
XLA Ops:
  7.2 0.0 copy-start
  7.2 0.0 reduce-scatter.3.cloned.1.call-start
  7.2 0.8 slice_bitcast_fusion.4
  8.0 0.9 select_reduce_fusion.2
  8.9 24.8 %all_gather.9 = bf16[2,16,8192]{2,1,0:T(8,128)(2,1)S(1)} all-gather(bf16[2,16,512]{2,1,0:T(8,128)(2,1)} %param.14), channel_id=1, replica_groups=mesh['groups'=2,'pool'=16] {'pool'}, dimensions={2}, use_global_device_ids=true | all-gather | bytes 557056 | tf_op jit(solution)/shard_map/all_gather | solution.py:86
  33.7 0.2 fusion.24
  34.0 2.1 fusion.14
  36.1 0.1 reduce_sum.90
  36.2 0.1 fusion.92
  36.3 0.1 multiply_multiply_fusion.1
  36.3 0.1 slice_multiply_fusion.5
  36.4 1.0 fusion.54
  37.5 1.7 fusion.58
  39.1 0.8 dynamic_slice.3
  39.9 1.6 fusion.38
  41.5 0.0 copy-start.6
  41.5 0.0 copy-start.1
  41.5 0.0 copy-start.4
  41.5 0.0 copy-start.5
  41.5 5.6 %convolution_add_fusion.1 = f32[16,10240]{1,0:T(8,128)S(1)} fusion(bf16[512,10240]{1,0:T(8,128)(2,1)} %param.16, f32[16,1024]{1,0:T(8,128)S(1)} %fusion.54, f32[16,1024]{1,0:T(8,128)} %fusion.58, f32[16,8192]{1,0:T(8,128)S(1)} %fusion.38, f32[16]{0:T(128)S(1)} %get-tuple-element.35, f32[512]{0:T(512)S(1)} %dynamic_slice.3, bf16[2,16,512]{2,1,0:T(8,128)(2,1)} %param.14), kind=kOutput, calls=%fused_computation.1 | convolution fusion | flops 168296448 | bytes 11814976 | tf_op jit(solution)/shard_map/dot_general | solution.py:117
  47.1 1.3 fusion.17
  48.4 0.1 reduce_sum.112
  48.5 0.1 multiply_multiply_fusion
  48.6 0.1 slice_multiply_fusion.2
  48.7 0.6 fusion.36
  49.3 0.2 fusion.52
  49.5 0.2 fusion.56
  49.7 0.0 copy-start.7
  49.7 5.5 %convolution_add_fusion = f32[16,10240]{1,0:T(8,128)S(1)} fusion(bf16[512,10240]{1,0:T(8,128)(2,1)} %param.16, f32[16,1024]{1,0:T(8,128)S(1)} %fusion.52, f32[16,1024]{1,0:T(8,128)S(1)} %fusion.56, f32[16,8192]{1,0:T(8,128)S(1)} %fusion.36, f32[16]{0:T(128)S(1)} %get-tuple-element.34, f32[512]{0:T(512)S(1)} %dynamic_slice.3, bf16[2,16,512]{2,1,0:T(8,128)(2,1)S(1)} %copy-done.5), kind=kOutput, calls=%fused_computation | convolution fusion | flops 168296448 | bytes 11815424 | tf_op jit(solution)/shard_map/dot_general | solution.py:117
  55.2 70.5 %all-reduce.4 = (bf16[16,10240]{1,0:T(8,128)(2,1)}, bf16[16,10240]{1,0:T(8,128)(2,1)}) all-reduce(f32[16,10240]{1,0:T(8,128)S(1)} %convolution_add_fusion, f32[16,10240]{1,0:T(8,128)S(1)} %convolution_add_fusion.1), channel_id=4, replica_groups=mesh['groups'=2,'pool'=16] {'pool'}, use_global_device_ids=true, to_apply=%region_10.11.clone | all-reduce | flops 327680 | bytes 1966080
  125.8 0.6 dynamic-slice
  126.4 1.6 dynamic-slice_convert_fusion.1
  128.0 0.1 slice_reduce_fusion.1
  128.1 0.1 fusion.79
  128.2 2.1 fusion.102
  130.3 0.2 copy.50
  131.1 0.3 fusion.105
  131.4 0.2 fusion.64
  131.6 1.3 copy.51
  132.9 0.3 fusion.11
  133.1 0.5 copy-done.3
  133.7 18.7 %all-gather = bf16[16,1,8192]{2,1,0:T(2,128)(2,1)S(1)} all-gather(bf16[1,1,8192]{2,1,0:T(2,128)(2,1)S(1)} %reshape.462), channel_id=1, replica_groups=mesh['groups'=2,'pool'=16] {'pool'}, dimensions={0}, use_global_device_ids=true | all-gather | bytes 278528 | tf_op jit(solution)/shard_map/all_gather | solution.py:128
  152.4 1.8 fusion.23
  154.1 2.4 fusion.32
  156.5 0.0 reduce-scatter.3.cloned.1.call-update
  156.6 0.0 reduce-scatter.5.cloned.1.call-start
  156.6 1.6 dynamic-slice_convert_fusion
  158.2 0.1 slice_reduce_fusion
  158.3 0.1 fusion.91
  158.4 0.3 fusion.103
  158.6 0.1 fusion.104
  158.8 0.2 fusion.65
  159.0 1.3 fusion.70
  160.3 0.2 fusion.9
  160.6 21.1 %all-gather.1 = bf16[16,1,8192]{2,1,0:T(2,128)(2,1)S(1)} all-gather(bf16[1,1,8192]{2,1,0:T(2,128)(2,1)S(1)} %reshape.464), channel_id=1, replica_groups=mesh['groups'=2,'pool'=16] {'pool'}, dimensions={0}, use_global_device_ids=true | all-gather | bytes 278528 | tf_op jit(solution)/shard_map/all_gather | solution.py:128
  181.7 0.7 fusion.21
  182.5 2.4 fusion.30
  184.9 0.0 reduce-scatter.5.cloned.1.call-update
  184.9 0.6 pad_maximum_fusion.2
  185.5 26.1 %reduce-scatter.3.cloned.1.call-done = f32[16,512]{1,0:T(8,128)} async-done(((f32[16,8192]{1,0:T(8,128)}), f32[16,512]{1,0:T(8,128)}) %reduce-scatter.3.cloned.1.call-update) | async-done | bytes 32784 | tf_op jit(solution)/shard_map/reduce_scatter | solution.py:140
  211.6 4.6 %fusion.13 = bf16[1,16,512]{2,1,0:T(8,128)(2,1)S(1)} fusion(f32[16,512]{1,0:T(8,128)} %reduce-scatter.3.cloned.1.call-done, bf16[8192,512]{1,0:T(8,128)(2,1)} %param.17, bf16[16,1,8192]{2,1,0:T(2,128)(2,1)S(1)} %all-gather, bf16[2,16,512]{2,1,0:T(8,128)(2,1)S(1)} %copy-done.5), kind=kOutput, calls=%fused_computation.21 | convolution fusion | flops 134250496 | bytes 8716288 | tf_op jit(solution)/shard_map/dot_general | solution.py:129
  216.2 54.3 %reduce-scatter.5.cloned.1.call-done = f32[16,512]{1,0:T(8,128)} async-done(((f32[16,8192]{1,0:T(8,128)}), f32[16,512]{1,0:T(8,128)}) %reduce-scatter.5.cloned.1.call-update) | async-done | bytes 32784 | tf_op jit(solution)/shard_map/reduce_scatter | solution.py:140
  270.5 4.6 %fusion.12 = bf16[1,16,512]{2,1,0:T(8,128)(2,1)S(1)} fusion(f32[16,512]{1,0:T(8,128)} %reduce-scatter.5.cloned.1.call-done, bf16[8192,512]{1,0:T(8,128)(2,1)} %param.17, bf16[16,1,8192]{2,1,0:T(2,128)(2,1)S(1)} %all-gather.1, bf16[2,16,512]{2,1,0:T(8,128)(2,1)S(1)} %copy-done.5), kind=kOutput, calls=%fused_computation.20 | convolution fusion | flops 134250496 | bytes 8716288 | tf_op jit(solution)/shard_map/dot_general | solution.py:129
  275.0 0.6 pad_maximum_fusion
  (24 shorter events, 0.2 us)
Async XLA Ops:
  7.2 26.8 %copy-start = (f32[1,48,8192]{2,1,0:T(8,128)S(1)}, f32[1,48,8192]{2,1,0:T(8,128)}, u32[]{:S(2)}) copy-start(f32[1,48,8192]{2,1,0:T(8,128)} %param.23) | copy-start | bytes 4718596
  7.2 204.4 %reduce-scatter.3.cloned.1.call-start = ((), (), s32[]{:S(2)}) async-start(), calls=%async_computation.2 | async-start | bytes 557056 | tf_op jit(solution)/shard_map/reduce_scatter | solution.py:140
  41.5 5.6 %copy-start.6 = (f32[8192]{0:T(1024)S(1)}, f32[8192]{0:T(1024)}, u32[]{:S(2)}) copy-start(f32[8192]{0:T(1024)} %param.15) | copy-start | bytes 98308
  41.5 7.2 %copy-start.1 = (f32[1,16,8192]{2,1,0:T(8,128)S(1)}, f32[1,16,8192]{2,1,0:T(8,128)}, u32[]{:S(2)}) copy-start(f32[1,16,8192]{2,1,0:T(8,128)} %param.24) | copy-start | bytes 1572868
  41.5 7.8 %copy-start.4 = (f32[1,2,16,1024]{3,2,1,0:T(8,128)S(1)}, f32[1,2,16,1024]{3,2,1,0:T(8,128)}, u32[]{:S(2)}) copy-start(f32[1,2,16,1024]{3,2,1,0:T(8,128)} %param.25) | copy-start | bytes 393220
  41.5 8.2 %copy-start.5 = (bf16[2,16,512]{2,1,0:T(8,128)(2,1)S(1)}, bf16[2,16,512]{2,1,0:T(8,128)(2,1)}, u32[]{:S(2)}) copy-start(bf16[2,16,512]{2,1,0:T(8,128)(2,1)} %param.14) | copy-start | bytes 98308
  49.7 76.0 %copy-start.7 = (u32[32]{0:T(128)S(1)}, u32[32]{0:T(128)}, u32[]{:S(2)}) copy-start(u32[32]{0:T(128)} %constant.39) | copy-start | bytes 388
  125.8 55.9 %copy-start.2 = (f32[1,16,8192]{2,1,0:T(8,128)S(1)}, f32[1,16,8192]{2,1,0:T(8,128)}, u32[]{:S(2)}) copy-start(f32[1,16,8192]{2,1,0:T(8,128)} %param.26) | copy-start | bytes 1572868
  132.9 0.8 copy-start.3
  156.6 113.9 %reduce-scatter.5.cloned.1.call-start = ((), (), s32[]{:S(2)}) async-start(), calls=%async_computation.3 | async-start | bytes 557056 | tf_op jit(solution)/shard_map/reduce_scatter | solution.py:140
Sparse Core Ops, SparseCore 0:
  156.7 54.8 reduce-scatter.2
  215.6 54.8 reduce-scatter.4
where the time goes:
time: 283 us; the launch traced here: 282 us
  blocking collectives  135 us (48%)
  waiting for transfers between devices  80.4 us (28%)
  matrix products  38.8 us (14%)
  between operations  15 us (5%)
  local copies, waits for them, and re-layouts  9.83 us (3%)
  other arithmetic  3.29 us (1%)
    reduce_scatter x2, waiting for transfers between devices, local(): lax.psum_scatter(complete_update, 'pool', scatter_dimension=1, tiled=True)  80.3 us
    unnamed x1, blocking collectives  70.5 us
    all_gather x2, blocking collectives, local(): lax.all_gather(attention_result, 'pool', axis=0, tiled=True)  39.9 us
    all_gather x1, blocking collectives, local(): gathered = lax.all_gather(hidden, 'pool', axis=2, tiled=True)  24.8 us
    dot_general x2, matrix products, local(): jnp.dot(normed, query_key_value_weight, preferred_element_type=jnp.float32)  11.1 us
    dot_general x8, matrix products, widen_rows(): jnp.dot(spread, factors.reshape(spread.shape[1], factors.shape[-1]), prec...  10.1 us
    dot_general x2, matrix products, local(): jnp.dot(out_block_rows, output_weight, preferred_element_type=jnp.float32)  9.15 us
  transfers between devices with their start and end apart: 2, of which 2 were waited for; matrix products, arithmetic and copies ran while one was open for 4% of the time, Pallas kernels for 0%

commit v1 on v0

v1 whole, which is shorter than its diff:
```python
import functools

import jax
import jax.numpy as jnp
from jax import lax
from jax.experimental import pallas as pl
from jax.experimental.pallas import tpu as pltpu
from jax.sharding import PartitionSpec as P

HEADS = 64
KV_HEADS = 8
HEAD_DIM = 128
GROUP = HEADS // KV_HEADS
STEPS = 2
RANK = 16
LANES = 128
CHUNK = 2 * KV_HEADS * HEAD_DIM
QUERY_CHUNKS = HEADS * HEAD_DIM // CHUNK
CHUNKS = QUERY_CHUNKS + 1
CHUNK_HEADS = CHUNK // HEAD_DIM
PACKED = CHUNK_HEADS * STEPS

epsilon = 1e-05
f32, bf16 = jnp.float32, jnp.bfloat16


def dot(a, b):
    return jnp.dot(a, b, preferred_element_type=f32)


def dot_t(a, b):
    return lax.dot_general(a, b, (((1,), (1,)), ((), ())), preferred_element_type=f32)


def split(a):
    high = a.astype(bf16)
    return high, (a - high.astype(f32)).astype(bf16)


def kernel(
    n,
    width,
    hid_ref,
    gain_ref,
    length_ref,
    index_ref,
    place_ref,
    rank_ref,
    wqkv_hbm,
    wout_hbm,
    cache_hbm,
    down_hbm,
    qup_hbm,
    kvup_hbm,
    odown_hbm,
    oup_hbm,
    out_ref,
    newkv_ref,
    wqkv,
    wout,
    cache,
    down,
    qup,
    kvup,
    odown,
    oup,
    down_split,
    odown_split,
    hid_all,
    normed_ref,
    part,
    core_out,
    core_in,
    half,
    y_out,
    y_in,
    quarter,
    z_rows,
    z_out,
    z_in,
    kv_rows,
    kv_flat,
    att_all,
    att_rows,
    att,
    oup_out,
    oup_in,
    small,
    load_sem,
    hid_send,
    hid_recv,
    att_send,
    att_recv,
    core_send,
    core_recv,
    y_send,
    y_recv,
    z_send,
    z_recv,
    oup_send,
    oup_recv,
    small_send,
    small_recv,
):
    me = lax.axis_index("pool")
    depth = n // 4
    my_z, my_y, my_core = me // 4, lax.rem(me // 2, 2), lax.rem(me, 2)
    rows = STEPS * n
    wd = width // n

    def at(z, y, core):
        return z * 4 + y * 2 + core

    core_peer = at(my_z, my_y, 1 - my_core)
    y_peer = at(my_z, 1 - my_y, my_core)

    def push(src, dst, send, recv, peer):
        return pltpu.make_async_remote_copy(
            src_ref=src,
            dst_ref=dst,
            send_sem=send,
            recv_sem=recv,
            device_id={"pool": peer},
            device_id_type=pl.DeviceIdType.MESH,
        )

    order = [QUERY_CHUNKS] + list(range(QUERY_CHUNKS))
    loads = [
        (down_hbm, down),
        (odown_hbm, odown),
        (oup_hbm, oup),
        (qup_hbm, qup),
        (kvup_hbm, kvup),
    ]
    loads += [(wqkv_hbm.at[:, pl.ds(c * CHUNK, CHUNK)], wqkv.at[c]) for c in order]
    loads += [(cache_hbm, cache), (wout_hbm, wout)]
    loads = [pltpu.make_async_copy(s, d, load_sem.at[i]) for i, (s, d) in enumerate(loads)]
    for load in loads:
        load.start()
    load_w = dict(zip(order, loads[5:]))
    load_cache, load_wout = loads[-2:]

    barrier = pltpu.get_barrier_semaphore()

    def greet(k, carry):
        pl.semaphore_signal(
            barrier,
            inc=1,
            device_id={"pool": lax.rem(me + k, n)},
            device_id_type=pl.DeviceIdType.MESH,
        )
        return carry

    lax.fori_loop(1, n, greet, 0)

    row = lax.broadcasted_iota(jnp.int32, (rows, rows), 0)
    column = lax.broadcasted_iota(jnp.int32, (rows, rows), 1)
    z_bits = depth.bit_length() - 1
    source = (
        (row & (STEPS - 1)) * n
        + ((row >> 1) & (depth - 1)) * 4
        + ((row >> (1 + z_bits)) & 1) * 2
        + (row >> (2 + z_bits))
    )
    order_rows = (source == column).astype(f32)
    hid_all[me] = dot(order_rows.astype(bf16), hid_ref[...]).astype(bf16)

    lane = lax.broadcasted_iota(jnp.int32, (rows, LANES), 1)
    adapters = place_ref.shape[1]
    matches = index_ref[...] == lax.broadcasted_iota(jnp.int32, (rows, adapters), 1)
    slot_of = jnp.sum(jnp.where(matches, place_ref[...].astype(f32), 0.0), axis=1, keepdims=True)
    rank_of = jnp.sum(jnp.where(matches, rank_ref[...].astype(f32), 0.0), axis=1, keepdims=True)
    keep = jnp.where(lane.astype(f32) < rank_of, 4.0 / jnp.sqrt(rank_of), 0.0)
    own_keep = jnp.where(slot_of == me.astype(f32), keep, 0.0)
    own_keep_ordered = jnp.dot(
        order_rows, own_keep, precision=lax.Precision.HIGHEST, preferred_element_type=f32
    )

    pl.semaphore_wait(barrier, n - 1)

    def gather(buffer, send, recv, use):
        started = []

        def start(block, peer):
            copy = push(buffer.at[block], buffer.at[block], send.at[len(started)], recv.at[block], peer)
            copy.start()
            started.append(copy)

        def arrived(block):
            push(buffer.at[block], buffer.at[block], send.at[0], recv.at[block], core_peer).wait_recv()

        for k in range(1, depth):
            start(me, at(lax.rem(my_z + k, depth), my_y, my_core))
        start(me, y_peer)
        start(me, core_peer)
        yield
        use(me)
        for k in range(1, depth):
            block = at(lax.rem(my_z + k, depth), my_y, my_core)
            arrived(block)
            start(block, y_peer)
            start(block, core_peer)
            use(block)
        for k in range(depth):
            block = at(lax.rem(my_z + k, depth), 1 - my_y, my_core)
            arrived(block)
            start(block, core_peer)
            use(block)
        for y in (my_y, 1 - my_y):
            for k in range(depth):
                block = at(lax.rem(my_z + k, depth), y, 1 - my_core)
                arrived(block)
                use(block)
        yield
        for copy in started:
            copy.wait_send()

    totals = [jnp.zeros((rows, 1), f32), jnp.zeros((rows, LANES), f32)]

    def use_hidden(block):
        values = hid_all[block]
        wide = values.astype(f32)
        totals[0] += jnp.sum(wide * wide, axis=1, keepdims=True)
        columns = pl.ds(pl.multiple_of(block * wd, wd), wd)
        totals[1] += dot_t(values, down_split[:, columns])

    hidden_gather = gather(hid_all, hid_send, hid_recv, use_hidden)
    next(hidden_gather)

    lora_rows = 3 * RANK
    down_split[2 * lora_rows :, :] = jnp.zeros((LANES - 2 * lora_rows, width), bf16)
    odown_split[2 * RANK :, :] = jnp.zeros((LANES - 2 * RANK, width), bf16)
    loads[0].wait()
    for start in range(0, width, 1024):
        columns = pl.ds(start, 1024)
        high, low = split(down[:, columns] * gain_ref[:, columns])
        down_split[:lora_rows, columns] = high
        down_split[lora_rows : 2 * lora_rows, columns] = low

    next(hidden_gather)

    loads[1].wait()
    loads[2].wait()
    for p in range(n):
        oup_out[p] = oup[:, p * wd : (p + 1) * wd].astype(bf16)
    mine = pl.ds(pl.multiple_of(me * RANK, RANK), RANK)
    oup_in[mine, :] = oup_out[me]

    def oup_copy(k):
        peer = lax.rem(me + k, n)
        return push(oup_out.at[peer], oup_in.at[mine, :], oup_send.at[k], oup_recv.at[me], peer)

    def start_oup(k, carry):
        oup_copy(k).start()
        return carry

    lax.fori_loop(1, n, start_oup, 0)

    inverse = lax.rsqrt(totals[0] * (1.0 / width) + epsilon)
    shrink = (totals[1] + pltpu.roll(totals[1], LANES - lora_rows, 1)) * inverse
    shrink_q = split((shrink * own_keep_ordered)[:, :RANK])
    shrink_k = split((pltpu.roll(shrink, LANES - RANK, 1) * own_keep_ordered)[:, :RANK])
    shrink_v = split((pltpu.roll(shrink, LANES - 2 * RANK, 1) * own_keep_ordered)[:, :RANK])
    gain_mine = gain_ref[:, pl.ds(pl.multiple_of(me * wd, wd), wd)]
    normed_ref[...] = (hid_all[me].astype(f32) * gain_mine * inverse).astype(bf16)
    loads[3].wait()
    loads[4].wait()

    def widen(shrunk, factors):
        high, low = split(factors)
        return dot(shrunk[0], high) + dot(shrunk[1], high) + dot(shrunk[0], low)

    rows_core, rows_y = rows // 2, rows // 4
    half_chunk = CHUNK // 2

    def core_copy(c):
        return push(core_out.at[c], core_in.at[c], core_send.at[c], core_recv.at[c], core_peer)

    def y_copy(c):
        return push(y_out.at[c], y_in.at[c], y_send.at[c], y_recv.at[c], y_peer)

    def z_copy(c, k):
        z = lax.rem(my_z + k, depth)
        return push(
            z_out.at[c, z],
            z_in.at[c, my_z],
            z_send.at[c, k],
            z_recv.at[c, my_z],
            at(z, my_y, my_core),
        )

    def project(c):
        load_w[c].wait()
        if c < QUERY_CHUNKS:
            lora = [(shrink_q, qup[:, c * CHUNK : (c + 1) * CHUNK], 0, CHUNK)]
        else:
            lora = [(shrink_k, kvup[0], 0, half_chunk), (shrink_v, kvup[1], half_chunk, half_chunk)]
        for shrunk, factors, first, size in lora:
            part[c, :, first : first + size] = dot(
                normed_ref[...], wqkv[c, :, first : first + size]
            ) + widen(shrunk, factors)
        other = pl.ds(pl.multiple_of((1 - my_core) * rows_core, rows_core), rows_core)
        core_out[c] = part[c, other, :].astype(bf16)
        core_copy(c).start()

    def add_core(c):
        core_copy(c).wait_recv()
        own = pl.ds(pl.multiple_of(my_core * rows_core, rows_core), rows_core)
        half[c] = part[c, own, :] + core_in[c].astype(f32)
        other = half[c, pl.ds(pl.multiple_of((1 - my_y) * rows_y, rows_y), rows_y), :]
        y_out[c] = jnp.concatenate([other[:, :half_chunk], other[:, half_chunk:]], axis=0).astype(bf16)
        y_copy(c).start()

    def add_y(c):
        y_copy(c).wait_recv()
        own = half[c, pl.ds(pl.multiple_of(my_y * rows_y, rows_y), rows_y), :]
        arrived = y_in[c].astype(f32)
        quarter[c, :, :half_chunk] = own[:, :half_chunk] + arrived[:rows_y]
        quarter[c, :, half_chunk:] = own[:, half_chunk:] + arrived[rows_y:]
        for z in range(depth):
            for j in range(CHUNK_HEADS):
                z_rows[c, z, STEPS * j : STEPS * (j + 1), :] = quarter[
                    c, STEPS * z : STEPS * (z + 1), HEAD_DIM * j : HEAD_DIM * (j + 1)
                ]
        z_out[c] = z_rows[c].astype(bf16)
        for k in range(1, depth):
            z_copy(c, k).start()

    def add_z(c):
        total = z_rows[c, my_z]
        for k in range(1, depth):
            z = lax.rem(my_z + k, depth)
            push(
                z_out.at[c, z], z_in.at[c, z], z_send.at[c, k], z_recv.at[c, z], core_peer
            ).wait_recv()
            total += z_in[c, z].astype(f32)
        return total.astype(bf16)

    for step in range(CHUNKS + 2):
        if step < CHUNKS:
            project(order[step])
        if 0 <= step - 1 < CHUNKS:
            add_core(order[step - 1])
        if 0 <= step - 2 < CHUNKS:
            add_y(order[step - 2])

    for start in range(0, width, 1024):
        columns = pl.ds(start, 1024)
        high, low = split(odown[:, columns])
        odown_split[:RANK, columns] = high
        odown_split[RANK : 2 * RANK, columns] = low

    load_cache.wait()
    kv_rows[...] = add_z(QUERY_CHUNKS).astype(f32)
    group_rows = GROUP * STEPS
    positions = cache.shape[0]
    scale = HEAD_DIM ** (-0.5)
    valid = lax.broadcasted_iota(jnp.int32, (group_rows, positions), 1) < length_ref[...]
    first_step = (lax.broadcasted_iota(jnp.int32, (group_rows, 1), 0) & (STEPS - 1)) == 0
    kv_width = KV_HEADS * HEAD_DIM
    for c in range(QUERY_CHUNKS):
        queries_all = add_z(c)
        for g in range(CHUNK_HEADS // GROUP):
            head = c * (CHUNK_HEADS // GROUP) + g
            queries = queries_all[g * group_rows : (g + 1) * group_rows]
            columns = slice(head * HEAD_DIM, (head + 1) * HEAD_DIM)
            value_columns = slice(kv_width + head * HEAD_DIM, kv_width + (head + 1) * HEAD_DIM)
            keys = [kv_rows[STEPS * head + t : STEPS * head + t + 1, :] for t in range(STEPS)]
            fresh_at = STEPS * (KV_HEADS + head)
            values = [kv_rows[fresh_at + t : fresh_at + t + 1, :] for t in range(STEPS)]
            scores = jnp.where(valid, dot_t(queries, cache[:, columns]) * scale, -1e30)
            wide = queries.astype(f32)
            fresh = [jnp.sum(wide * key, axis=1, keepdims=True) * scale for key in keys]
            fresh[1] = jnp.where(first_step, -1e30, fresh[1])
            top = jnp.maximum(jnp.max(scores, axis=1, keepdims=True), jnp.maximum(*fresh))
            exps = jnp.exp(scores - top)
            fresh = [jnp.exp(s - top) for s in fresh]
            total = jnp.sum(exps, axis=1, keepdims=True) + fresh[0] + fresh[1]
            result = dot((exps / total).astype(bf16), cache[:, value_columns])
            for s, value in zip(fresh, values):
                result += (s / total).astype(bf16).astype(f32) * value
            att_all[me, pl.ds(head * group_rows, group_rows), :] = result.astype(bf16)

    att_block = HEADS * STEPS

    def use_attended(block):
        att_rows[pl.ds(pl.multiple_of(block * att_block, att_block), att_block), :] = att_all[
            block
        ].astype(f32)

    attended_gather = gather(att_all, att_send, att_recv, use_attended)
    next(attended_gather)
    for t in range(STEPS):
        for j in range(CHUNK_HEADS):
            kv_flat[t : t + 1, HEAD_DIM * j : HEAD_DIM * (j + 1)] = kv_rows[
                STEPS * j + t : STEPS * j + t + 1, :
            ]
    newkv_ref[...] = kv_flat[...].astype(bf16)
    next(attended_gather)

    for h in range(HEADS):
        for t in range(STEPS):
            att[t * n : (t + 1) * n, h * HEAD_DIM : (h + 1) * HEAD_DIM] = att_rows[
                pl.ds(STEPS * h + t, n, stride=att_block), :
            ].astype(bf16)

    shrunk = dot_t(att[...], odown_split[...])
    shrunk = (shrunk + pltpu.roll(shrunk, LANES - RANK, 1)) * own_keep
    spots = LANES // RANK
    packed = []
    for q in range(max(1, rows // (8 * spots))):
        groups = min(spots, rows // 8 - q * spots)
        total = jnp.zeros((8, LANES), f32)
        for g in range(groups):
            first = 8 * (q * spots + g)
            piece = shrunk[first : first + 8]
            total += piece if g == 0 else pltpu.roll(piece, RANK * g, 1)
        packed.append(total)
    small[me] = packed[0] if len(packed) == 1 else jnp.concatenate(packed, axis=0)

    def small_copy(k):
        peer = lax.rem(me + k, n)
        return push(small.at[me], small.at[me], small_send.at[k], small_recv.at[me], peer)

    def start_small(k, carry):
        small_copy(k).start()
        return carry

    lax.fori_loop(1, n, start_small, 0)

    load_wout.wait()
    base = dot(att[...], wout[...]) + hid_ref[...].astype(f32)

    def end_oup(k, carry):
        other = lax.rem(me + k, n)
        theirs = pl.ds(pl.multiple_of(other * RANK, RANK), RANK)
        push(
            oup_out.at[other], oup_in.at[theirs, :], oup_send.at[k], oup_recv.at[other], other
        ).wait()
        return carry

    lax.fori_loop(1, n, end_oup, 0)

    def end_small(k, carry):
        other = lax.rem(me + k, n)
        push(small.at[other], small.at[other], small_send.at[k], small_recv.at[other], other).wait()
        return carry

    lax.fori_loop(1, n, end_small, 0)

    whole = small[0]
    for p in range(1, n):
        whole += small[p]
    pieces = []
    for i in range(rows // 8):
        q, g = divmod(i, spots)
        piece = whole[8 * q : 8 * q + 8]
        pieces.append(piece if g == 0 else pltpu.roll(piece, LANES - RANK * g, 1))
    rows_out = jnp.where(lane < RANK, jnp.concatenate(pieces, axis=0), 0.0)
    reach = RANK
    while reach < LANES:
        rows_out += pltpu.roll(rows_out, reach, 1)
        reach *= 2
    spread = jnp.concatenate([rows_out] * (n * RANK // LANES), axis=1)
    place_of = lax.broadcasted_iota(jnp.int32, (rows, n * RANK), 1) >> (RANK.bit_length() - 1)
    high, low = split(jnp.where(place_of.astype(f32) == slot_of, spread, 0.0))
    update = dot(high, oup_in[...]) + dot(low, oup_in[...])
    out_ref[...] = (base + update).astype(bf16)

    for gathered in (hidden_gather, attended_gather):
        for _ in gathered:
            pass
    for c in range(CHUNKS):
        core_copy(c).wait_send()
        y_copy(c).wait_send()
        for k in range(1, depth):
            z_copy(c, k).wait_send()


def local(
    n,
    hidden,
    norm_gain_vector,
    query_key_value_weight,
    output_weight,
    key_value_cache,
    cache_valid_length,
    request_adapter_index,
    adapter_slot_place,
    adapter_rank_used,
    adapter_down_factor,
    query_up_factor,
    key_value_up_factor,
    output_down_factor,
    output_up_factor,
):
    steps, requests, wd = hidden.shape
    width = norm_gain_vector.shape[0]
    positions = key_value_cache.shape[1]
    assert steps == STEPS and requests == n and adapter_down_factor.shape[0] == 1 and wd * n == width
    rows, depth = steps * n, n // 4
    att_block = HEADS * STEPS
    sends = 4 * depth
    packed_rows = 8 * max(1, rows * RANK // (8 * LANES))
    vmem = pl.BlockSpec(memory_space=pltpu.VMEM)
    hbm = pl.BlockSpec(memory_space=pl.ANY)
    dma = pltpu.SemaphoreType.DMA
    out, new_kv = pl.pallas_call(
        functools.partial(kernel, n, width),
        out_shape=(
            jax.ShapeDtypeStruct((rows, wd), bf16),
            jax.ShapeDtypeStruct((STEPS, CHUNK), bf16),
        ),
        in_specs=[vmem] * 6 + [hbm] * 8,
        out_specs=(vmem, vmem),
        scratch_shapes=[
            pltpu.VMEM((CHUNKS, wd, CHUNK), bf16),
            pltpu.VMEM((width, wd), bf16),
            pltpu.VMEM((positions, CHUNK), bf16),
            pltpu.VMEM((3 * RANK, width), f32),
            pltpu.VMEM((RANK, width), f32),
            pltpu.VMEM((2, RANK, CHUNK // 2), f32),
            pltpu.VMEM((RANK, width), f32),
            pltpu.VMEM((RANK, width), f32),
            pltpu.VMEM((LANES, width), bf16),
            pltpu.VMEM((LANES, width), bf16),
            pltpu.VMEM((n, rows, wd), bf16),
            pltpu.VMEM((rows, wd), bf16),
            pltpu.VMEM((CHUNKS, rows, CHUNK), f32),
            pltpu.VMEM((CHUNKS, rows // 2, CHUNK), bf16),
            pltpu.VMEM((CHUNKS, rows // 2, CHUNK), bf16),
            pltpu.VMEM((CHUNKS, rows // 2, CHUNK), f32),
            pltpu.VMEM((CHUNKS, rows // 2, CHUNK // 2), bf16),
            pltpu.VMEM((CHUNKS, rows // 2, CHUNK // 2), bf16),
            pltpu.VMEM((CHUNKS, rows // 4, CHUNK), f32),
            pltpu.VMEM((CHUNKS, depth, PACKED, HEAD_DIM), f32),
            pltpu.VMEM((CHUNKS, depth, PACKED, HEAD_DIM), bf16),
            pltpu.VMEM((CHUNKS, depth, PACKED, HEAD_DIM), bf16),
            pltpu.VMEM((PACKED, HEAD_DIM), f32),
            pltpu.VMEM((STEPS, CHUNK), f32),
            pltpu.VMEM((n, att_block, HEAD_DIM), bf16),
            pltpu.VMEM((n * att_block, HEAD_DIM), f32),
            pltpu.VMEM((rows, HEADS * HEAD_DIM), bf16),
            pltpu.VMEM((n, RANK, wd), bf16),
            pltpu.VMEM((n * RANK, wd), bf16),
            pltpu.VMEM((n, packed_rows, LANES), f32),
            dma((5 + CHUNKS + 2,)),
            dma((sends,)),
            dma((n,)),
            dma((sends,)),
            dma((n,)),
            dma((CHUNKS,)),
            dma((CHUNKS,)),
            dma((CHUNKS,)),
            dma((CHUNKS,)),
            dma((CHUNKS, depth)),
            dma((CHUNKS, depth)),
            dma((n,)),
            dma((n,)),
            dma((n,)),
            dma((n,)),
        ],
        compiler_params=pltpu.CompilerParams(
            collective_id=0, has_side_effects=True, vmem_limit_bytes=56 * 1024 * 1024
        ),
        cost_estimate=pl.CostEstimate(
            flops=2 * rows * 18 * 1024 * width // n * 8, bytes_accessed=24 << 20, transcendentals=0
        ),
    )(
        hidden.reshape(rows, wd),
        norm_gain_vector.reshape(1, width),
        cache_valid_length.reshape(1, 1),
        request_adapter_index.reshape(rows, 1),
        adapter_slot_place.reshape(1, -1),
        adapter_rank_used.reshape(1, -1),
        query_key_value_weight,
        output_weight,
        key_value_cache.reshape(positions, CHUNK),
        adapter_down_factor.reshape(3 * RANK, width),
        query_up_factor.reshape(RANK, width),
        key_value_up_factor.reshape(2, RANK, CHUNK // 2),
        output_down_factor.reshape(RANK, width),
        output_up_factor.reshape(RANK, width),
    )
    return out.reshape(steps, requests, wd), new_kv.reshape(steps, 1, CHUNK)


def solution(mesh):
    placed = (
        P(None, "groups", "pool"),
        P(),
        P("pool", None),
        P(None, "pool"),
        P(("groups", "pool"), None, None),
        P(("groups", "pool")),
        P(None, "groups", None),
        P("groups"),
        P("groups"),
        P(("groups", "pool"), None, None),
        P(("groups", "pool"), None, None),
        P(("groups", "pool"), None, None, None),
        P(("groups", "pool"), None, None),
        P(("groups", "pool"), None, None),
    )
    return jax.shard_map(
        functools.partial(local, mesh.shape["pool"]),
        mesh=mesh,
        in_specs=placed,
        out_specs=(P(None, "groups", "pool"), P(None, ("groups", "pool"), None)),
        check_vma=False,
    )
```

time: 283 us -> 56.7 us (0.20)
  blocking collectives: 135 us -> 0 us
  waiting for transfers between devices: 80.4 us -> 0 us
  Pallas kernels: 0 us -> 49.8 us
  matrix products: 38.8 us -> 0 us
  between operations: 15 us -> 1.29 us
  local copies, waits for them, and re-layouts: 9.83 us -> 3.89 us
    reduce_scatter x2 -> x0, waiting for transfers between devices: 80.3 us -> none  [local(): lax.psum_scatter(complete_update, 'pool', scatter_dimension=1, tiled=True)]
    unnamed x1 -> x0, blocking collectives: 70.5 us -> none
    all_gather x3 -> x0, blocking collectives: 64.6 us -> none  [the longest x2 39.9 us: local(): lax.all_gather(attention_result, 'pool', axis=0, tiled=True)]
    pallas_call x0 -> x1, Pallas kernels: none -> 49.8 us  [local(): pl.pallas_call(functools.partial(kernel, n, width), out_shape=(jax.ShapeD...]
    dot_general x23 -> x0, matrix products: 38.8 us -> none  [the longest x2 11.1 us: local(): jnp.dot(normed, query_key_value_weight, preferred_element_type=jnp.float32)]
    another operation x4 -> x0, local copies, waits for them, and re-layouts: 3.24 us -> none
  transfers between devices with their start and end apart: 2 -> 0, of which waited for: 2 -> 0; matrix products, arithmetic and copies ran while one was open for 4% -> 0% of each run, Pallas kernels for 0% -> 0%
where the time goes in v1:
time: 56.7 us; the launch traced here: 56.3 us
  Pallas kernels  49.8 us (88%)
  local copies, waits for them, and re-layouts  3.89 us (7%)
  other arithmetic  1.34 us (2%)
  between operations  1.29 us (2%)
    pallas_call x1, Pallas kernels, local(): pl.pallas_call(functools.partial(kernel, n, width), out_shape=(jax.ShapeD...  49.8 us
    unnamed x3, local copies, waits for them, and re-layouts  3.19 us
    unnamed x1, other arithmetic  1.34 us

profile of v1, /device:TPU:0, one launch (start us, length us, event | category | flops | bytes accessed | tf_op | source)
XLA Modules:
  0.0 56.3 jit_solution(15932859375792444575)
XLA Ops:
  1.3 0.5 broadcast.3
  1.8 1.3 %reduce.3 = s32[2,16]{1,0:T(2,128)S(1)} reduce(s32[2,16,1]{1,2,0:T(1,128)} %param.20, s32[]{:T(128)} %broadcast.3), dimensions={2}, to_apply=%param.20.reduce_sub_computation.3 | reduce | bytes 260 | tf_op args[6]
  3.1 0.7 %reshape.60.index_ref = s32[32,1]{1,0:T(8,128)} reshape(s32[2,16]{1,0:T(2,128)S(1)} %reduce.3) | data formatting | bytes 256 | tf_op jit(solution)/shard_map/reshape | solution.py:573
  3.8 49.8 %shard_map.149 = (bf16[32,512]{1,0:T(8,128)(2,1)}, bf16[2,2048]{1,0:T(2,128)(2,1)}) custom-call(bf16[32,512]{1,0:T(8,128)(2,1)} %bitcast.21, f32[1,8192]{1,0:T(1,128)} %bitcast.22, s32[1,1]{1,0:T(1,128)} %bitcast.14.length_ref, s32[32,1]{1,0:T(8,128)} %reshape.60.index_ref, s32[1,16]{1,0:T(1,128)} %bitcast.25, s32[1,16]{1,0:T(1,128)} %bitcast.26, ...), custom_call_target="tpu_custom_call" | custom-call | flops 4831838208 | bytes 25165824 | tf_op jit(solution)/shard_map/pallas_call | solution.py:508
  53.7 1.4 %copy.20 = bf16[2,16,512]{2,1,0:T(8,128)(2,1)} copy(bf16[2,16,512]{2,1,0:T(8,128)(2,1)} %bitcast.23) | data formatting | bytes 65536
  55.0 1.3 %copy.21 = bf16[2,1,2048]{2,0,1:T(2,128)(2,1)} copy(bf16[2,1,2048]{2,0,1:T(2,128)(2,1)} %bitcast.24) | data formatting | bytes 16384

commit v2 on v1

--- a/solution.py
+++ b/solution.py
@@ -167,7 +167,16 @@
 
     lane = lax.broadcasted_iota(jnp.int32, (rows, LANES), 1)
     adapters = place_ref.shape[1]
-    matches = index_ref[...] == lax.broadcasted_iota(jnp.int32, (rows, adapters), 1)
+    same = lax.broadcasted_iota(jnp.int32, (n, n), 0) == lax.broadcasted_iota(jnp.int32, (n, n), 1)
+    adapter_of = jnp.concatenate(
+        [
+            jnp.sum(jnp.where(same, index_ref[t].astype(f32), 0.0), axis=1, keepdims=True)
+            for t in range(STEPS)
+        ],
+        axis=0,
+    )
+    adapter = lax.broadcasted_iota(jnp.int32, (rows, adapters), 1)
+    matches = adapter_of == adapter.astype(f32)
     slot_of = jnp.sum(jnp.where(matches, place_ref[...].astype(f32), 0.0), axis=1, keepdims=True)
     rank_of = jnp.sum(jnp.where(matches, rank_ref[...].astype(f32), 0.0), axis=1, keepdims=True)
     keep = jnp.where(lane.astype(f32) < rank_of, 4.0 / jnp.sqrt(rank_of), 0.0)
@@ -227,6 +236,22 @@
     hidden_gather = gather(hid_all, hid_send, hid_recv, use_hidden)
     next(hidden_gather)
 
+    loads[2].wait()
+    for p in range(n):
+        oup_out[p] = oup[:, p * wd : (p + 1) * wd].astype(bf16)
+    mine = pl.ds(pl.multiple_of(me * RANK, RANK), RANK)
+    oup_in[mine, :] = oup_out[me]
+
+    def oup_copy(k):
+        peer = lax.rem(me + k, n)
+        return push(oup_out.at[peer], oup_in.at[mine, :], oup_send.at[k], oup_recv.at[me], peer)
+
+    def start_oup(k, carry):
+        oup_copy(k).start()
+        return carry
+
+    lax.fori_loop(1, n, start_oup, 0)
+
     lora_rows = 3 * RANK
     down_split[2 * lora_rows :, :] = jnp.zeros((LANES - 2 * lora_rows, width), bf16)
     odown_split[2 * RANK :, :] = jnp.zeros((LANES - 2 * RANK, width), bf16)
@@ -238,23 +263,6 @@
         down_split[lora_rows : 2 * lora_rows, columns] = low
 
     next(hidden_gather)
-
-    loads[1].wait()
-    loads[2].wait()
-    for p in range(n):
-        oup_out[p] = oup[:, p * wd : (p + 1) * wd].astype(bf16)
-    mine = pl.ds(pl.multiple_of(me * RANK, RANK), RANK)
-    oup_in[mine, :] = oup_out[me]
-
-    def oup_copy(k):
-        peer = lax.rem(me + k, n)
-        return push(oup_out.at[peer], oup_in.at[mine, :], oup_send.at[k], oup_recv.at[me], peer)
-
-    def start_oup(k, carry):
-        oup_copy(k).start()
-        return carry
-
-    lax.fori_loop(1, n, start_oup, 0)
 
     inverse = lax.rsqrt(totals[0] * (1.0 / width) + epsilon)
     shrink = (totals[1] + pltpu.roll(totals[1], LANES - lora_rows, 1)) * inverse
@@ -336,14 +344,15 @@
             total += z_in[c, z].astype(f32)
         return total.astype(bf16)
 
-    for step in range(CHUNKS + 2):
+    for step in range(CHUNKS + 4):
         if step < CHUNKS:
             project(order[step])
-        if 0 <= step - 1 < CHUNKS:
-            add_core(order[step - 1])
         if 0 <= step - 2 < CHUNKS:
-            add_y(order[step - 2])
-
+            add_core(order[step - 2])
+        if 0 <= step - 4 < CHUNKS:
+            add_y(order[step - 4])
+
+    loads[1].wait()
     for start in range(0, width, 1024):
         columns = pl.ds(start, 1024)
         high, low = split(odown[:, columns])
@@ -475,6 +484,11 @@
         y_copy(c).wait_send()
         for k in range(1, depth):
             z_copy(c, k).wait_send()
+
+
+def hand_over(rows_ref, kv_ref, rows_out, kv_out):
+    rows_out[...] = rows_ref[...]
+    kv_out[...] = kv_ref[...]
 
 
 def local(
@@ -570,7 +584,7 @@
         hidden.reshape(rows, wd),
         norm_gain_vector.reshape(1, width),
         cache_valid_length.reshape(1, 1),
-        request_adapter_index.reshape(rows, 1),
+        request_adapter_index.transpose(0, 2, 1),
         adapter_slot_place.reshape(1, -1),
         adapter_rank_used.reshape(1, -1),
         query_key_value_weight,
@@ -582,6 +596,15 @@
         output_down_factor.reshape(RANK, width),
         output_up_factor.reshape(RANK, width),
     )
+    out, new_kv = pl.pallas_call(
+        hand_over,
+        out_shape=(
+            jax.ShapeDtypeStruct((rows, wd), bf16),
+            jax.ShapeDtypeStruct((STEPS, CHUNK), bf16),
+        ),
+        in_specs=[vmem, vmem],
+        out_specs=(vmem, vmem),
+    )(out, new_kv)
     return out.reshape(steps, requests, wd), new_kv.reshape(steps, 1, CHUNK)
 
 

time: 56.7 us -> 51.7 us (0.912)
  local copies, waits for them, and re-layouts: 3.89 us -> 0 us
  other arithmetic: 1.34 us -> 0 us
    unnamed x3 -> x0, local copies, waits for them, and re-layouts: 3.19 us -> none
    pallas_call x0 -> x1, Pallas kernels: none -> 1.38 us  [local(): pl.pallas_call(hand_over, out_shape=(jax.ShapeDtypeStruct((rows, wd), bf1...]
    unnamed x1 -> x0, other arithmetic: 1.34 us -> none
    pallas_call x1, Pallas kernels: 49.8 us -> 48.7 us  [local(): pl.pallas_call(functools.partial(kernel, n, width), out_shape=(jax.ShapeD...]
    reshape x1 -> x0, local copies, waits for them, and re-layouts: 0.7 us -> none  [local(): request_adapter_index.reshape(rows, 1)]
where the time goes in v2:
time: 51.7 us; the launch traced here: 51.4 us
  Pallas kernels  50.1 us (97%)
  between operations  1.29 us (2%)
    pallas_call x1, Pallas kernels, local(): pl.pallas_call(functools.partial(kernel, n, width), out_shape=(jax.ShapeD...  48.7 us
    pallas_call x1, Pallas kernels, local(): pl.pallas_call(hand_over, out_shape=(jax.ShapeDtypeStruct((rows, wd), bf1...  1.38 us

profile of v2, /device:TPU:0, one launch (start us, length us, event | category | flops | bytes accessed | tf_op | source)
XLA Modules:
  0.0 51.4 jit_solution(15905814664328369486)
XLA Ops:
  1.3 48.7 %shard_map.149 = (bf16[32,512]{1,0:T(8,128)(2,1)}, bf16[2,2048]{1,0:T(2,128)(2,1)}) custom-call(bf16[32,512]{1,0:T(8,128)(2,1)} %bitcast.23, f32[1,8192]{1,0:T(1,128)} %bitcast.24, s32[1,1]{1,0:T(1,128)} %bitcast.16.length_ref, s32[2,1,16]{2,1,0:T(1,128)} %bitcast.25, s32[1,16]{1,0:T(1,128)} %bitcast.26, s32[1,16]{1,0:T(1,128)} %bitcast.27, ...), custom_call_target="tpu_custom_call" | custom-call | flops 4831838208 | bytes 25165824 | tf_op jit(solution)/shard_map/pallas_call | solution.py:522
  50.0 1.4 %shard_map.150 = (bf16[32,512]{1,0:T(8,128)(2,1)}, bf16[2,2048]{1,0:T(2,128)(2,1)}) custom-call(bf16[32,512]{1,0:T(8,128)(2,1)} %get-tuple-element.6.rows_ref, bf16[2,2048]{1,0:T(2,128)(2,1)} %get-tuple-element.7.kv_ref), custom_call_target="tpu_custom_call" | custom-call | tf_op jit(solution)/shard_map/pallas_call | solution.py:599

commit v3 on v2

--- a/solution.py
+++ b/solution.py
@@ -111,6 +111,13 @@
     def at(z, y, core):
         return z * 4 + y * 2 + core
 
+    def paired(k):
+        z = my_z
+        for bit in range(depth.bit_length() - 1):
+            if k >> bit & 1:
+                z = z + (1 << bit) * (1 - 2 * lax.rem(z // (1 << bit), 2))
+        return z
+
     core_peer = at(my_z, my_y, 1 - my_core)
     y_peer = at(my_z, 1 - my_y, my_core)
 
@@ -157,8 +164,8 @@
     column = lax.broadcasted_iota(jnp.int32, (rows, rows), 1)
     z_bits = depth.bit_length() - 1
     source = (
-        (row & (STEPS - 1)) * n
-        + ((row >> 1) & (depth - 1)) * 4
+        ((row >> z_bits) & (STEPS - 1)) * n
+        + (row & (depth - 1)) * 4
         + ((row >> (1 + z_bits)) & 1) * 2
         + (row >> (2 + z_bits))
     )
@@ -185,6 +192,33 @@
         order_rows, own_keep, precision=lax.Precision.HIGHEST, preferred_element_type=f32
     )
 
+    lora_rows = 3 * RANK
+    down_split[2 * lora_rows :, :] = jnp.zeros((LANES - 2 * lora_rows, width), bf16)
+    loads[0].wait()
+    for start in range(0, width, 1024):
+        columns = pl.ds(start, 1024)
+        high, low = split(down[:, columns] * gain_ref[:, columns])
+        down_split[:lora_rows, columns] = high
+        down_split[lora_rows : 2 * lora_rows, columns] = low
+
+    loads[1].wait()
+    for start in range(0, width, 1024):
+        high, low = split(odown[:, pl.ds(start, 1024)])
+        stacked = jnp.concatenate(
+            [high.astype(f32), low.astype(f32), jnp.zeros((LANES - 2 * RANK, 1024), f32)], axis=0
+        )
+        odown_split[pl.ds(start, 1024), :] = stacked.T.astype(bf16)
+
+    loads[2].wait()
+    for p in range(n):
+        oup_out[p] = oup[:, p * wd : (p + 1) * wd].astype(bf16)
+    mine = pl.ds(pl.multiple_of(me * RANK, RANK), RANK)
+    oup_in[mine, :] = oup_out[me]
+
+    def oup_copy(k):
+        peer = lax.rem(me + k, n)
+        return push(oup_out.at[peer], oup_in.at[mine, :], oup_send.at[k], oup_recv.at[me], peer)
+
     pl.semaphore_wait(barrier, n - 1)
 
     def gather(buffer, send, recv, use):
@@ -198,26 +232,26 @@
         def arrived(block):
             push(buffer.at[block], buffer.at[block], send.at[0], recv.at[block], core_peer).wait_recv()
 
-        for k in range(1, depth):
-            start(me, at(lax.rem(my_z + k, depth), my_y, my_core))
+        for k in range(depth - 1, 0, -1):
+            start(me, at(paired(k), my_y, my_core))
         start(me, y_peer)
         start(me, core_peer)
         yield
         use(me)
         for k in range(1, depth):
-            block = at(lax.rem(my_z + k, depth), my_y, my_core)
+            block = at(paired(k), my_y, my_core)
             arrived(block)
             start(block, y_peer)
             start(block, core_peer)
             use(block)
         for k in range(depth):
-            block = at(lax.rem(my_z + k, depth), 1 - my_y, my_core)
+            block = at(paired(k), 1 - my_y, my_core)
             arrived(block)
             start(block, core_peer)
             use(block)
         for y in (my_y, 1 - my_y):
             for k in range(depth):
-                block = at(lax.rem(my_z + k, depth), y, 1 - my_core)
+                block = at(paired(k), y, 1 - my_core)
                 arrived(block)
                 use(block)
         yield
@@ -235,32 +269,12 @@
 
     hidden_gather = gather(hid_all, hid_send, hid_recv, use_hidden)
     next(hidden_gather)
-
-    loads[2].wait()
-    for p in range(n):
-        oup_out[p] = oup[:, p * wd : (p + 1) * wd].astype(bf16)
-    mine = pl.ds(pl.multiple_of(me * RANK, RANK), RANK)
-    oup_in[mine, :] = oup_out[me]
-
-    def oup_copy(k):
-        peer = lax.rem(me + k, n)
-        return push(oup_out.at[peer], oup_in.at[mine, :], oup_send.at[k], oup_recv.at[me], peer)
-
     def start_oup(k, carry):
         oup_copy(k).start()
         return carry
 
     lax.fori_loop(1, n, start_oup, 0)
 
-    lora_rows = 3 * RANK
-    down_split[2 * lora_rows :, :] = jnp.zeros((LANES - 2 * lora_rows, width), bf16)
-    odown_split[2 * RANK :, :] = jnp.zeros((LANES - 2 * RANK, width), bf16)
-    loads[0].wait()
-    for start in range(0, width, 1024):
-        columns = pl.ds(start, 1024)
-        high, low = split(down[:, columns] * gain_ref[:, columns])
-        down_split[:lora_rows, columns] = high
-        down_split[lora_rows : 2 * lora_rows, columns] = low
 
     next(hidden_gather)
 
@@ -288,7 +302,7 @@
         return push(y_out.at[c], y_in.at[c], y_send.at[c], y_recv.at[c], y_peer)
 
     def z_copy(c, k):
-        z = lax.rem(my_z + k, depth)
+        z = paired(k)
         return push(
             z_out.at[c, z],
             z_in.at[c, my_z],
@@ -325,19 +339,19 @@
         arrived = y_in[c].astype(f32)
         quarter[c, :, :half_chunk] = own[:, :half_chunk] + arrived[:rows_y]
         quarter[c, :, half_chunk:] = own[:, half_chunk:] + arrived[rows_y:]
-        for z in range(depth):
+        for t in range(STEPS):
             for j in range(CHUNK_HEADS):
-                z_rows[c, z, STEPS * j : STEPS * (j + 1), :] = quarter[
-                    c, STEPS * z : STEPS * (z + 1), HEAD_DIM * j : HEAD_DIM * (j + 1)
+                z_rows[c, pl.ds(STEPS * j + t, depth, stride=PACKED), :] = quarter[
+                    c, depth * t : depth * (t + 1), HEAD_DIM * j : HEAD_DIM * (j + 1)
                 ]
-        z_out[c] = z_rows[c].astype(bf16)
+        z_out[c] = z_rows[c].reshape(depth, PACKED, HEAD_DIM).astype(bf16)
+        for k in range(depth - 1, 0, -1):
+            z_copy(c, k).start()
+
+    def add_z(c):
+        total = z_rows[c, pl.ds(pl.multiple_of(my_z * PACKED, PACKED), PACKED), :]
         for k in range(1, depth):
-            z_copy(c, k).start()
-
-    def add_z(c):
-        total = z_rows[c, my_z]
-        for k in range(1, depth):
-            z = lax.rem(my_z + k, depth)
+            z = paired(k)
             push(
                 z_out.at[c, z], z_in.at[c, z], z_send.at[c, k], z_recv.at[c, z], core_peer
             ).wait_recv()
@@ -351,13 +365,6 @@
             add_core(order[step - 2])
         if 0 <= step - 4 < CHUNKS:
             add_y(order[step - 4])
-
-    loads[1].wait()
-    for start in range(0, width, 1024):
-        columns = pl.ds(start, 1024)
-        high, low = split(odown[:, columns])
-        odown_split[:RANK, columns] = high
-        odown_split[RANK : 2 * RANK, columns] = low
 
     load_cache.wait()
     kv_rows[...] = add_z(QUERY_CHUNKS).astype(f32)
@@ -413,7 +420,7 @@
                 pl.ds(STEPS * h + t, n, stride=att_block), :
             ].astype(bf16)
 
-    shrunk = dot_t(att[...], odown_split[...])
+    shrunk = dot(att[...], odown_split[...])
     shrunk = (shrunk + pltpu.roll(shrunk, LANES - RANK, 1)) * own_keep
     spots = LANES // RANK
     packed = []
@@ -537,7 +544,7 @@
             pltpu.VMEM((RANK, width), f32),
             pltpu.VMEM((RANK, width), f32),
             pltpu.VMEM((LANES, width), bf16),
-            pltpu.VMEM((LANES, width), bf16),
+            pltpu.VMEM((width, LANES), bf16),
             pltpu.VMEM((n, rows, wd), bf16),
             pltpu.VMEM((rows, wd), bf16),
             pltpu.VMEM((CHUNKS, rows, CHUNK), f32),
@@ -547,7 +554,7 @@
             pltpu.VMEM((CHUNKS, rows // 2, CHUNK // 2), bf16),
             pltpu.VMEM((CHUNKS, rows // 2, CHUNK // 2), bf16),
             pltpu.VMEM((CHUNKS, rows // 4, CHUNK), f32),
-            pltpu.VMEM((CHUNKS, depth, PACKED, HEAD_DIM), f32),
+            pltpu.VMEM((CHUNKS, depth * PACKED, HEAD_DIM), f32),
             pltpu.VMEM((CHUNKS, depth, PACKED, HEAD_DIM), bf16),
             pltpu.VMEM((CHUNKS, depth, PACKED, HEAD_DIM), bf16),
             pltpu.VMEM((PACKED, HEAD_DIM), f32),

time: 51.7 us -> 51.5 us (level)
  no operation moved by 1% of the time
where the time goes in v3:
time: 51.5 us; the launch traced here: 51.3 us
  Pallas kernels  50 us (97%)
  between operations  1.29 us (3%)
    pallas_call x1, Pallas kernels, local(): pl.pallas_call(functools.partial(kernel, n, width), out_shape=(jax.ShapeD...  48.6 us
    pallas_call x1, Pallas kernels, local(): pl.pallas_call(hand_over, out_shape=(jax.ShapeDtypeStruct((rows, wd), bf1...  1.38 us

profile of v3, /device:TPU:0, one launch (start us, length us, event | category | flops | bytes accessed | tf_op | source)
XLA Modules:
  0.0 51.3 jit_solution(7461581371219219069)
XLA Ops:
  1.3 48.6 %shard_map.149 = (bf16[32,512]{1,0:T(8,128)(2,1)}, bf16[2,2048]{1,0:T(2,128)(2,1)}) custom-call(bf16[32,512]{1,0:T(8,128)(2,1)} %bitcast.23, f32[1,8192]{1,0:T(1,128)} %bitcast.24, s32[1,1]{1,0:T(1,128)} %bitcast.16.length_ref, s32[2,1,16]{2,1,0:T(1,128)} %bitcast.25, s32[1,16]{1,0:T(1,128)} %bitcast.26, s32[1,16]{1,0:T(1,128)} %bitcast.27, ...), custom_call_target="tpu_custom_call" | custom-call | flops 4831838208 | bytes 25165824 | tf_op jit(solution)/shard_map/pallas_call | solution.py:529
  49.9 1.4 %shard_map.150 = (bf16[32,512]{1,0:T(8,128)(2,1)}, bf16[2,2048]{1,0:T(2,128)(2,1)}) custom-call(bf16[32,512]{1,0:T(8,128)(2,1)} %get-tuple-element.6.rows_ref, bf16[2,2048]{1,0:T(2,128)(2,1)} %get-tuple-element.7.kv_ref), custom_call_target="tpu_custom_call" | custom-call | tf_op jit(solution)/shard_map/pallas_call | solution.py:606
